TPU v7x, 32 devices: a whole 2x2x4 slice. The times are simulated.
32 devices in a mesh: groups: 2 (over y), date: 4 (over z), rng: 2 (over x), az: 2 (over core).
Axes of the slice: x: 2, y: 2, z: 4, core: 2. Of those that a mesh axis runs over, the one named last changes fastest.
Arguments:
- slc: bfloat16 [2, 8, 64, 5120], P(None, ('groups', 'date'), 'az', 'rng'), parts along dimension 1, may hold values from -24 to 24
- offsets: int32 [8, 2], P(('groups', 'date')), parts along dimension 0, may hold values from -24 to 24, as said below
- kernel_index: int32 [8, 2], P(('groups', 'date')), parts along dimension 0, may hold values from 0 to 15
- range_shift: float32 [8], P('groups'), parts along dimension 0, may hold values from -0.15 to 0.15
Outputs:
- ifg: float32 [2, 8, 8, 16, 256], P(None, ('groups', 'date'), None, 'az', 'rng'), parts along dimension 1
There are 2 independent parts, one for each index of `groups`. A program takes and returns all parts, laid end to end along the dimension named above; each array names one. Nothing has to cross between parts.
Inputs may be any that keep to these rules, and one draw needn't show every extreme that they name: `offsets`: column 0 is the azimuth offset, within -8 to 8; column 1 is the range offset. Both ends of both ranges are taken by some date.
All inputs are finite; a program needn't handle non-finite values.
Results may differ from a plain program's by a relative error of at most 0.0039.
Values may be sent and summed in bfloat16 or wider, within the bound.
No kernel may reach another device: no remote copies, remote signals or barrier semaphores. Data moves between devices by JAX's collectives and lax.ppermute only.
A program may use at most 64 MiB of HBM per device.

v0:
```python
import jax
import jax.numpy as jnp
from jax import lax
from jax.sharding import PartitionSpec as P

LAGS = 8
KERNELS = 16
FILTER_HALF = 8
LOOK_AZ = 4
LOOK_RG = 20
HALO_AZ = 12
HALO_RG = 36


def padded(cells, sides, width):
    for axis, dim in sides:
        count = lax.axis_size(axis)
        ends = count - 1
        head = lax.slice_in_dim(cells, 0, width, axis=dim)
        tail = lax.slice_in_dim(cells, cells.shape[dim] - width, cells.shape[dim], axis=dim)
        cells = jnp.concatenate(
            [
                lax.ppermute(tail, axis, [(i, (i + 1) % count) for i in range(ends)]),
                cells,
                lax.ppermute(head, axis, [((i + 1) % count, i) for i in range(ends)]),
            ],
            axis=dim,
        )
    return cells


def shifted(value, axis, steps):
    count = lax.axis_size(axis)
    leading, last = (max(0, -steps), min(count, count - steps))
    return lax.ppermute(value, axis, [(source, source + steps) for source in range(leading, last)])


def kernel_taps(index):
    fraction = index.astype(jnp.float32) / KERNELS
    position = jnp.arange(8, dtype=jnp.float32) - 3.0 - fraction
    shaped = jnp.sinc(position) * (0.5 + 0.5 * jnp.cos(jnp.pi * position / 5.0))
    return shaped / jnp.sum(shaped)


def lowpass_taps(band_gap):
    spacing = jnp.arange(2 * FILTER_HALF + 1, dtype=jnp.float32) - FILTER_HALF
    window = (
        0.4
        * jnp.sinc(0.4 * spacing)
        * (0.54 + 0.46 * jnp.cos(jnp.pi * spacing / (FILTER_HALF + 1)))
    )
    phase_angle = jnp.pi * band_gap * spacing
    return (window * jnp.cos(phase_angle), window * jnp.sin(phase_angle))


def resample(source, shift_pair, kernel_pair, line_count, column_count):
    span_width = column_count + 2 * FILTER_HALF
    line_start = HALO_AZ + shift_pair[0] - 3
    column_start = HALO_RG - FILTER_HALF + shift_pair[1] - 3
    window = lax.dynamic_slice(
        source, (jnp.int32(0), line_start, column_start), (2, line_count + 7, span_width + 7)
    ).astype(jnp.float32)
    column_taps = kernel_taps(kernel_pair[1])
    line_taps = kernel_taps(kernel_pair[0])
    across = sum((column_taps[q] * window[:, :, q : q + span_width] for q in range(8)))
    return sum((line_taps[p] * across[:, p : p + line_count, :] for p in range(8))).astype(
        jnp.bfloat16
    )


def spectral_gap(range_shift, own_date, other_date):
    own_value = lax.dynamic_index_in_dim(range_shift, own_date, 0, keepdims=False)
    other_value = lax.dynamic_index_in_dim(range_shift, other_date, 0, keepdims=False)
    return own_value - other_value


def pair_looks(master, partner, band_gap):
    cos_taps, sin_taps = lowpass_taps(band_gap)
    column_count = master.shape[-1] - 2 * FILTER_HALF
    line_count = master.shape[1]
    master_re = jnp.zeros((line_count, column_count), jnp.float32)
    master_im = master_re
    partner_re = master_re
    partner_im = master_re
    for t in range(2 * FILTER_HALF + 1):
        first_part = master[:, :, t : t + column_count].astype(jnp.float32)
        second_part = partner[:, :, t : t + column_count].astype(jnp.float32)
        master_re = master_re + cos_taps[t] * first_part[0] + sin_taps[t] * first_part[1]
        master_im = master_im + cos_taps[t] * first_part[1] - sin_taps[t] * first_part[0]
        partner_re = partner_re + cos_taps[t] * second_part[0] - sin_taps[t] * second_part[1]
        partner_im = partner_im + cos_taps[t] * second_part[1] + sin_taps[t] * second_part[0]
    product = jnp.stack(
        [
            master_re * partner_re + master_im * partner_im,
            master_im * partner_re - master_re * partner_im,
        ]
    )
    blocks = product.reshape(2, line_count // LOOK_AZ, LOOK_AZ, column_count // LOOK_RG, LOOK_RG)
    return jnp.mean(blocks, axis=(2, 4))


def shifted_pairs(
    arrived, resampled, range_shift, first_date, date_total, per_device, line_count, padded_width
):
    gathered = jnp.concatenate(arrived, axis=1)

    def one_pair(pair_index):
        within = pair_index // LAGS
        later = within + pair_index % LAGS + 1
        master = lax.dynamic_index_in_dim(resampled, within, 1, keepdims=False)
        partner = lax.dynamic_index_in_dim(gathered, later, 1, keepdims=False).reshape(
            2, line_count, padded_width
        )
        chosen = jnp.minimum(first_date + later, date_total - 1)
        band_gap = spectral_gap(range_shift, first_date + within, chosen)
        return pair_looks(master, partner, band_gap)

    looks = lax.map(one_pair, jnp.arange(per_device * LAGS, dtype=jnp.int32))
    looks = looks.reshape((per_device, LAGS) + looks.shape[1:])
    return jnp.transpose(looks, (2, 0, 1, 3, 4))


def body(slc, offsets, kernel_index, range_shift):
    with_lines = padded(slc, (("az", 2),), HALO_AZ)
    widened = padded(with_lines, (("rng", 3),), HALO_RG)
    per_device = slc.shape[1]
    line_count = slc.shape[2]
    column_count = slc.shape[3]
    padded_width = column_count + 2 * FILTER_HALF
    date_devices = lax.axis_size("date")
    first_date = lax.axis_index("date") * per_device
    date_total = date_devices * per_device
    resampled = jnp.stack(
        [resample(widened[:, 0], offsets[0], kernel_index[0], line_count, column_count)], axis=1
    )
    packed = resampled.reshape(2, per_device, line_count * padded_width)
    device_reach = (per_device - 1 + LAGS) // per_device
    arrived = [packed]
    current = packed
    for hop_count in range(device_reach):
        current = shifted(current, "date", -1)
        arrived.append(current)
    return shifted_pairs(
        arrived,
        resampled,
        range_shift,
        first_date,
        date_total,
        per_device,
        line_count,
        padded_width,
    )


def solution(mesh):
    return jax.shard_map(
        body,
        mesh=mesh,
        in_specs=(
            P(None, ("groups", "date"), "az", "rng"),
            P(("groups", "date"), None),
            P(("groups", "date"), None),
            P("groups"),
        ),
        out_specs=P(None, ("groups", "date"), None, "az", "rng"),
        check_vma=False,
    )
```

profile of v0, /device:TPU:0, one launch (start us, length us, event | category | flops | bytes accessed | tf_op | source)
XLA Modules:
  0.0 516.0 jit_solution(12337977733939594580)
XLA Ops:
  12.7 4.2 collective-permute-start.2
  23.7 6.6 %fusion.7 = f32[2,39,2576]{2,1,0:T(8,128)S(1)} fusion(f32[2,39,2583]{2,1,0:T(8,128)S(1)} %bitcast_convert_fusion, f32[]{:T(128)} %bitcast.55, f32[]{:T(128)} %bitcast.54, f32[]{:T(128)} %bitcast.53, f32[]{:T(128)} %bitcast.52, f32[]{:T(128)} %bitcast.51, f32[]{:T(128)} %bitcast.50, f32[]{:T(128)} %bitcast.48, f32[]{:T(128)} %bitcast.41), kind=kLoop, calls=%fused_computation.64 | loop fusion | flops 3013920 | bytes 7233440 | tf_op jit(solution)/shard_map/add | solution.py:65
  30.3 5.5 %fusion.15 = bf16[2,32,2576]{2,1,0:T(8,128)(2,1)S(1)} fusion(f32[2,39,2576]{2,1,0:T(8,128)S(1)} %fusion.7, f32[]{:T(128)} %bitcast.62, f32[]{:T(128)} %bitcast.61, f32[]{:T(128)} %bitcast.60, f32[]{:T(128)} %bitcast.59, f32[]{:T(128)} %bitcast.58, f32[]{:T(128)} %bitcast.57, f32[]{:T(128)} %bitcast.56, f32[]{:T(128)} %bitcast.39), kind=kLoop, calls=%fused_computation.80 | loop fusion | flops 2637824 | bytes 5605408 | tf_op jit(solution)/shard_map/convert_element_type | solution.py:66
  38.0 5.5 %fusion.43 = bf16[2,1,32,2576]{3,2,0,1:T(8,128)(2,1)S(1)} fusion(f32[2,39,2576]{2,1,0:T(8,128)S(1)} %fusion.7, f32[]{:T(128)} %bitcast.62, f32[]{:T(128)} %bitcast.61, f32[]{:T(128)} %bitcast.60, f32[]{:T(128)} %bitcast.59, f32[]{:T(128)} %bitcast.58, f32[]{:T(128)} %bitcast.57, f32[]{:T(128)} %bitcast.56, f32[]{:T(128)} %bitcast.39), kind=kLoop, calls=%fused_computation.147 | loop fusion | flops 2637824 | bytes 5605408 | tf_op jit(solution)/shard_map/stack | solution.py:133
  43.5 4.8 collective-permute-done.4
  49.9 9.2 %collective-permute-done.5 = bf16[2,1,82432]{2,0,1:T(2,128)(2,1)S(1)} collective-permute-done((bf16[2,1,82432]{2,0,1:T(2,128)(2,1)S(1)}, bf16[2,1,82432]{2,0,1:T(2,128)(2,1)S(1)}, u32[]{:S(2)}, u32[]{:S(2)}) %collective-permute-start.5) | collective-permute-done | bytes 329760 | tf_op jit(solution)/shard_map/ppermute | solution.py:35
  60.7 8.3 %collective-permute-done.6 = bf16[2,1,82432]{2,0,1:T(2,128)(2,1)S(1)} collective-permute-done((bf16[2,1,82432]{2,0,1:T(2,128)(2,1)S(1)}, bf16[2,1,82432]{2,0,1:T(2,128)(2,1)S(1)}, u32[]{:S(2)}, u32[]{:S(2)}) %collective-permute-start.6) | collective-permute-done | bytes 329760 | tf_op jit(solution)/shard_map/ppermute | solution.py:35
  70.6 7.4 %collective-permute-done.7 = bf16[2,1,82432]{2,0,1:T(2,128)(2,1)S(1)} collective-permute-done((bf16[2,1,82432]{2,0,1:T(2,128)(2,1)S(1)}, bf16[2,1,82432]{2,0,1:T(2,128)(2,1)S(1)}, u32[]{:S(2)}, u32[]{:S(2)}) %collective-permute-start.7) | collective-permute-done | bytes 329760 | tf_op jit(solution)/shard_map/ppermute | solution.py:35
  79.5 7.8 %collective-permute-done.8 = bf16[2,1,82432]{2,0,1:T(2,128)(2,1)S(1)} collective-permute-done((bf16[2,1,82432]{2,0,1:T(2,128)(2,1)S(1)}, bf16[2,1,82432]{2,0,1:T(2,128)(2,1)S(1)}, u32[]{:S(2)}, u32[]{:S(2)}) %collective-permute-start.8) | collective-permute-done | bytes 329760 | tf_op jit(solution)/shard_map/ppermute | solution.py:35
  88.9 8.8 %collective-permute-done.9 = bf16[2,1,82432]{2,0,1:T(2,128)(2,1)S(1)} collective-permute-done((bf16[2,1,82432]{2,0,1:T(2,128)(2,1)S(1)}, bf16[2,1,82432]{2,0,1:T(2,128)(2,1)S(1)}, u32[]{:S(2)}, u32[]{:S(2)}) %collective-permute-start.9) | collective-permute-done | bytes 329760 | tf_op jit(solution)/shard_map/ppermute | solution.py:35
  99.3 10.0 %collective-permute-done.10 = bf16[2,1,82432]{2,0,1:T(2,128)(2,1)S(1)} collective-permute-done((bf16[2,1,82432]{2,0,1:T(2,128)(2,1)S(1)}, bf16[2,1,82432]{2,0,1:T(2,128)(2,1)S(1)}, u32[]{:S(2)}, u32[]{:S(2)}) %collective-permute-start.10) | collective-permute-done | bytes 329760 | tf_op jit(solution)/shard_map/ppermute | solution.py:35
  111.0 7.2 %collective-permute-done.11 = bf16[2,1,82432]{2,0,1:T(2,128)(2,1)S(1)} collective-permute-done((bf16[2,1,82432]{2,0,1:T(2,128)(2,1)S(1)}, bf16[2,1,82432]{2,0,1:T(2,128)(2,1)S(1)}, u32[]{:S(2)}, u32[]{:S(2)}) %collective-permute-start.11) | collective-permute-done | bytes 329760 | tf_op jit(solution)/shard_map/ppermute | solution.py:35
  120.1 395.2 %while.12 = (s32[]{:T(128)}, f32[8,2,8,128]{3,2,0,1:T(8,128)S(1)}, s32[8]{0:T(128)S(1)}, s32[]{:T(128)}, f32[4]{0:T(128)S(1)}, /*index=5*/bf16[2,1,32,2576]{3,2,...) while((s32[]{:T(128)}, f32[8,2,8,128]{3,2,0,1:T(8,128)S(1)}, ...), condition=%wide.region_4.6_spmd, body=%wide.region_2.5_spmd.sunk | while | flops 28345088 | bytes 97682888 | solution.py:118
  124.7 5.0 slice_convert_fusion.36
  133.3 2.5 slice_convert_fusion.37
  136.8 26.3 %multiply_add_fusion.9 = (f32[1,32,2560]{2,1,0:T(8,128)S(1)}, f32[1,32,2560]{2,1,0:T(8,128)S(1)}, f32[1,32,2560]{2,1,0:T(8,128)S(1)}, f32[1,32,2560]{2,1,0:T(8,128)S(1)}, f32[1,32,2560]{2,1,0:T(8,128)S(1)}) fusion(f32[2,32,2560]{2,1,0:T(8,128)S(1)} %get-tuple-element.339, f32[]{:T(128)} %bitcast.115, f32[]{:T(128)} %bitcast.116, ...), kind=kLoop, calls=%fused_computation.36.clone.1 | loop fusion | flops 22200320 | bytes 23920776 | tf_op jit(solution)/shard_map/while/body/eval_jaxpr/add | solution.py:94
  163.2 2.4 stack.15
  166.3 2.4 stack.16
  174.1 5.0 slice_convert_fusion.36
  182.7 2.5 slice_convert_fusion.37
  186.2 26.3 %multiply_add_fusion.9 = (f32[1,32,2560]{2,1,0:T(8,128)S(1)}, f32[1,32,2560]{2,1,0:T(8,128)S(1)}, f32[1,32,2560]{2,1,0:T(8,128)S(1)}, f32[1,32,2560]{2,1,0:T(8,128)S(1)}, f32[1,32,2560]{2,1,0:T(8,128)S(1)}) fusion(f32[2,32,2560]{2,1,0:T(8,128)S(1)} %get-tuple-element.339, f32[]{:T(128)} %bitcast.115, f32[]{:T(128)} %bitcast.116, ...), kind=kLoop, calls=%fused_computation.36.clone.1 | loop fusion | flops 22200320 | bytes 23920776 | tf_op jit(solution)/shard_map/while/body/eval_jaxpr/add | solution.py:94
  215.7 2.4 stack.16
  223.5 5.0 slice_convert_fusion.36
  232.1 2.5 slice_convert_fusion.37
  235.6 26.3 %multiply_add_fusion.9 = (f32[1,32,2560]{2,1,0:T(8,128)S(1)}, f32[1,32,2560]{2,1,0:T(8,128)S(1)}, f32[1,32,2560]{2,1,0:T(8,128)S(1)}, f32[1,32,2560]{2,1,0:T(8,128)S(1)}, f32[1,32,2560]{2,1,0:T(8,128)S(1)}) fusion(f32[2,32,2560]{2,1,0:T(8,128)S(1)} %get-tuple-element.339, f32[]{:T(128)} %bitcast.115, f32[]{:T(128)} %bitcast.116, ...), kind=kLoop, calls=%fused_computation.36.clone.1 | loop fusion | flops 22200320 | bytes 23920776 | tf_op jit(solution)/shard_map/while/body/eval_jaxpr/add | solution.py:94
  265.1 2.4 stack.16
  272.9 5.0 slice_convert_fusion.36
  281.5 2.5 slice_convert_fusion.37
  285.0 26.3 %multiply_add_fusion.9 = (f32[1,32,2560]{2,1,0:T(8,128)S(1)}, f32[1,32,2560]{2,1,0:T(8,128)S(1)}, f32[1,32,2560]{2,1,0:T(8,128)S(1)}, f32[1,32,2560]{2,1,0:T(8,128)S(1)}, f32[1,32,2560]{2,1,0:T(8,128)S(1)}) fusion(f32[2,32,2560]{2,1,0:T(8,128)S(1)} %get-tuple-element.339, f32[]{:T(128)} %bitcast.115, f32[]{:T(128)} %bitcast.116, ...), kind=kLoop, calls=%fused_computation.36.clone.1 | loop fusion | flops 22200320 | bytes 23920776 | tf_op jit(solution)/shard_map/while/body/eval_jaxpr/add | solution.py:94
  314.5 2.4 stack.16
  322.3 5.0 slice_convert_fusion.36
  330.9 2.5 slice_convert_fusion.37
  334.4 26.3 %multiply_add_fusion.9 = (f32[1,32,2560]{2,1,0:T(8,128)S(1)}, f32[1,32,2560]{2,1,0:T(8,128)S(1)}, f32[1,32,2560]{2,1,0:T(8,128)S(1)}, f32[1,32,2560]{2,1,0:T(8,128)S(1)}, f32[1,32,2560]{2,1,0:T(8,128)S(1)}) fusion(f32[2,32,2560]{2,1,0:T(8,128)S(1)} %get-tuple-element.339, f32[]{:T(128)} %bitcast.115, f32[]{:T(128)} %bitcast.116, ...), kind=kLoop, calls=%fused_computation.36.clone.1 | loop fusion | flops 22200320 | bytes 23920776 | tf_op jit(solution)/shard_map/while/body/eval_jaxpr/add | solution.py:94
  360.8 2.4 stack.15
  363.9 2.4 stack.16
  371.7 5.0 slice_convert_fusion.36
  380.3 2.5 slice_convert_fusion.37
  383.9 26.3 %multiply_add_fusion.9 = (f32[1,32,2560]{2,1,0:T(8,128)S(1)}, f32[1,32,2560]{2,1,0:T(8,128)S(1)}, f32[1,32,2560]{2,1,0:T(8,128)S(1)}, f32[1,32,2560]{2,1,0:T(8,128)S(1)}, f32[1,32,2560]{2,1,0:T(8,128)S(1)}) fusion(f32[2,32,2560]{2,1,0:T(8,128)S(1)} %get-tuple-element.339, f32[]{:T(128)} %bitcast.115, f32[]{:T(128)} %bitcast.116, ...), kind=kLoop, calls=%fused_computation.36.clone.1 | loop fusion | flops 22200320 | bytes 23920776 | tf_op jit(solution)/shard_map/while/body/eval_jaxpr/add | solution.py:94
  410.2 2.4 stack.15
  413.3 2.4 stack.16
  421.1 5.0 slice_convert_fusion.36
  429.7 2.5 slice_convert_fusion.37
  433.3 26.3 %multiply_add_fusion.9 = (f32[1,32,2560]{2,1,0:T(8,128)S(1)}, f32[1,32,2560]{2,1,0:T(8,128)S(1)}, f32[1,32,2560]{2,1,0:T(8,128)S(1)}, f32[1,32,2560]{2,1,0:T(8,128)S(1)}, f32[1,32,2560]{2,1,0:T(8,128)S(1)}) fusion(f32[2,32,2560]{2,1,0:T(8,128)S(1)} %get-tuple-element.339, f32[]{:T(128)} %bitcast.115, f32[]{:T(128)} %bitcast.116, ...), kind=kLoop, calls=%fused_computation.36.clone.1 | loop fusion | flops 22200320 | bytes 23920776 | tf_op jit(solution)/shard_map/while/body/eval_jaxpr/add | solution.py:94
  462.7 2.4 stack.16
  470.5 5.0 slice_convert_fusion.36
  479.1 2.5 slice_convert_fusion.37
  482.7 26.3 %multiply_add_fusion.9 = (f32[1,32,2560]{2,1,0:T(8,128)S(1)}, f32[1,32,2560]{2,1,0:T(8,128)S(1)}, f32[1,32,2560]{2,1,0:T(8,128)S(1)}, f32[1,32,2560]{2,1,0:T(8,128)S(1)}, f32[1,32,2560]{2,1,0:T(8,128)S(1)}) fusion(f32[2,32,2560]{2,1,0:T(8,128)S(1)} %get-tuple-element.339, f32[]{:T(128)} %bitcast.115, f32[]{:T(128)} %bitcast.116, ...), kind=kLoop, calls=%fused_computation.36.clone.1 | loop fusion | flops 22200320 | bytes 23920776 | tf_op jit(solution)/shard_map/while/body/eval_jaxpr/add | solution.py:94
  512.1 2.4 stack.16
  (355 shorter events, 98.9 us)
Async XLA Ops:
  1.0 10.4 %collective-permute-start = (bf16[2,1,12,2560]{3,2,0,1:T(8,128)(2,1)S(1)}, bf16[2,1,12,2560]{3,2,0,1:T(8,128)(2,1)S(1)}, u32[]{:S(2)}, u32[]{:S(2)}) collective-permute-start(bf16[2,1,12,2560]{3,2,0,1:T(8,128)(2,1)S(1)} %get-tuple-element.197), channel_id=1, source_target_pairs={{0,1},{2,3},{4,5},{6,7},{8,9},{10,11},{12,13},{14,15},{16,17},{18,... | collective-permute-start | bytes 368648 | tf_op jit(solution)/shard_map/ppermute | solution.py:23
  3.4 8.0 %collective-permute-start.1 = (bf16[2,1,12,2560]{3,2,0,1:T(8,128)(2,1)S(1)}, bf16[2,1,12,2560]{3,2,0,1:T(8,128)(2,1)S(1)}, u32[]{:S(2)}, u32[]{:S(2)}) collective-permute-start(bf16[2,1,12,2560]{3,2,0,1:T(8,128)(2,1)S(1)} %get-tuple-element.198), channel_id=1, source_target_pairs={{1,0},{3,2},{5,4},{7,6},{9,8},{11,10},{13,12},{15,14},{17,16},{19,... | collective-permute-start | bytes 368648 | tf_op jit(solution)/shard_map/ppermute | solution.py:25
  12.7 9.4 %collective-permute-start.2 = (bf16[2,1,56,36]{3,2,0,1:T(8,128)(2,1)S(1)}, bf16[2,1,56,36]{3,2,0,1:T(8,128)(2,1)S(1)}, u32[]{:S(2)}, u32[]{:S(2)}) collective-permute-start(bf16[2,1,56,36]{3,2,0,1:T(8,128)(2,1)S(1)} %get-tuple-element.196), channel_id=1, source_target_pairs={{0,2},{1,3},{4,6},{5,7},{8,10},{9,11},{12,14},{13,15},{16,18},{17,... | collective-permute-start | bytes 24200 | tf_op jit(solution)/shard_map/ppermute | solution.py:23
  16.9 6.0 %collective-permute-start.3 = (bf16[2,1,56,36]{3,2,0,1:T(8,128)(2,1)S(1)}, bf16[2,1,56,36]{3,2,0,1:T(8,128)(2,1)S(1)}, u32[]{:S(2)}, u32[]{:S(2)}) collective-permute-start(bf16[2,1,56,36]{3,2,0,1:T(8,128)(2,1)S(1)} %get-tuple-element.195), channel_id=1, source_target_pairs={{2,0},{3,1},{6,4},{7,5},{10,8},{11,9},{14,12},{15,13},{18,16},{19,... | collective-permute-start | bytes 24200 | tf_op jit(solution)/shard_map/ppermute | solution.py:25
  36.7 11.6 %collective-permute-start.4 = (bf16[2,1,82432]{2,0,1:T(2,128)(2,1)S(1)}, bf16[2,1,82432]{2,0,1:T(2,128)(2,1)S(1)}, u32[]{:S(2)}, u32[]{:S(2)}) collective-permute-start(bf16[2,1,82432]{2,0,1:T(2,128)(2,1)S(1)} %reshape_stack.3), channel_id=1, source_target_pairs={{4,0},{8,4},{12,8},{5,1},{9,5},{13,9},{6,2},{10,6},{14,10},{7,3},{... | collective-permute-start | bytes 989192 | tf_op jit(solution)/shard_map/ppermute | solution.py:35
  43.5 76.6 %copy-start.14 = (f32[4]{0:T(128)S(1)}, f32[4]{0:T(128)}, u32[]{:S(2)}) copy-start(f32[4]{0:T(128)} %param.10) | copy-start | bytes 52
  48.3 10.8 %collective-permute-start.5 = (bf16[2,1,82432]{2,0,1:T(2,128)(2,1)S(1)}, bf16[2,1,82432]{2,0,1:T(2,128)(2,1)S(1)}, u32[]{:S(2)}, u32[]{:S(2)}) collective-permute-start(bf16[2,1,82432]{2,0,1:T(2,128)(2,1)S(1)} %collective-permute-done.4), channel_id=1, source_target_pairs={{4,0},{8,4},{12,8},{5,1},{9,5},{13,9},{6,2},{10,6},{14,10},{7,3},{... | collective-permute-start | bytes 989192 | tf_op jit(solution)/shard_map/ppermute | solution.py:35
  59.1 9.9 %collective-permute-start.6 = (bf16[2,1,82432]{2,0,1:T(2,128)(2,1)S(1)}, bf16[2,1,82432]{2,0,1:T(2,128)(2,1)S(1)}, u32[]{:S(2)}, u32[]{:S(2)}) collective-permute-start(bf16[2,1,82432]{2,0,1:T(2,128)(2,1)S(1)} %collective-permute-done.5), channel_id=1, source_target_pairs={{4,0},{8,4},{12,8},{5,1},{9,5},{13,9},{6,2},{10,6},{14,10},{7,3},{... | collective-permute-start | bytes 989192 | tf_op jit(solution)/shard_map/ppermute | solution.py:35
  69.0 9.0 %collective-permute-start.7 = (bf16[2,1,82432]{2,0,1:T(2,128)(2,1)S(1)}, bf16[2,1,82432]{2,0,1:T(2,128)(2,1)S(1)}, u32[]{:S(2)}, u32[]{:S(2)}) collective-permute-start(bf16[2,1,82432]{2,0,1:T(2,128)(2,1)S(1)} %collective-permute-done.6), channel_id=1, source_target_pairs={{4,0},{8,4},{12,8},{5,1},{9,5},{13,9},{6,2},{10,6},{14,10},{7,3},{... | collective-permute-start | bytes 989192 | tf_op jit(solution)/shard_map/ppermute | solution.py:35
  78.0 9.3 %collective-permute-start.8 = (bf16[2,1,82432]{2,0,1:T(2,128)(2,1)S(1)}, bf16[2,1,82432]{2,0,1:T(2,128)(2,1)S(1)}, u32[]{:S(2)}, u32[]{:S(2)}) collective-permute-start(bf16[2,1,82432]{2,0,1:T(2,128)(2,1)S(1)} %collective-permute-done.7), channel_id=1, source_target_pairs={{4,0},{8,4},{12,8},{5,1},{9,5},{13,9},{6,2},{10,6},{14,10},{7,3},{... | collective-permute-start | bytes 989192 | tf_op jit(solution)/shard_map/ppermute | solution.py:35
  87.3 10.4 %collective-permute-start.9 = (bf16[2,1,82432]{2,0,1:T(2,128)(2,1)S(1)}, bf16[2,1,82432]{2,0,1:T(2,128)(2,1)S(1)}, u32[]{:S(2)}, u32[]{:S(2)}) collective-permute-start(bf16[2,1,82432]{2,0,1:T(2,128)(2,1)S(1)} %collective-permute-done.8), channel_id=1, source_target_pairs={{4,0},{8,4},{12,8},{5,1},{9,5},{13,9},{6,2},{10,6},{14,10},{7,3},{... | collective-permute-start | bytes 989192 | tf_op jit(solution)/shard_map/ppermute | solution.py:35
  97.7 11.6 %collective-permute-start.10 = (bf16[2,1,82432]{2,0,1:T(2,128)(2,1)S(1)}, bf16[2,1,82432]{2,0,1:T(2,128)(2,1)S(1)}, u32[]{:S(2)}, u32[]{:S(2)}) collective-permute-start(bf16[2,1,82432]{2,0,1:T(2,128)(2,1)S(1)} %collective-permute-done.9), channel_id=1, source_target_pairs={{4,0},{8,4},{12,8},{5,1},{9,5},{13,9},{6,2},{10,6},{14,10},{7,3},{... | collective-permute-start | bytes 989192 | tf_op jit(solution)/shard_map/ppermute | solution.py:35
  109.3 9.0 %collective-permute-start.11 = (bf16[2,1,82432]{2,0,1:T(2,128)(2,1)S(1)}, bf16[2,1,82432]{2,0,1:T(2,128)(2,1)S(1)}, u32[]{:S(2)}, u32[]{:S(2)}) collective-permute-start(bf16[2,1,82432]{2,0,1:T(2,128)(2,1)S(1)} %collective-permute-done.10), channel_id=1, source_target_pairs={{4,0},{8,4},{12,8},{5,1},{9,5},{13,9},{6,2},{10,6},{14,10},{7,3},{... | collective-permute-start | bytes 989192 | tf_op jit(solution)/shard_map/ppermute | solution.py:35
  133.2 2.7 copy-start.8
  133.2 3.0 copy-start.9
  133.2 3.2 copy-start.10
  133.3 3.4 copy-start.11
  133.3 3.6 copy-start.12
  182.6 2.7 copy-start.8
  182.6 3.0 copy-start.9
  182.6 3.2 copy-start.10
  182.7 3.4 copy-start.11
  182.7 3.6 copy-start.12
  232.0 2.7 copy-start.8
  232.0 3.0 copy-start.9
  232.1 3.2 copy-start.10
  232.1 3.4 copy-start.11
  232.1 3.6 copy-start.12
  281.4 3.0 copy-start.9
  281.5 3.2 copy-start.10
  281.5 3.4 copy-start.11
  281.5 3.6 copy-start.12
  330.9 3.0 copy-start.9
  330.9 3.2 copy-start.10
  330.9 3.4 copy-start.11
  330.9 3.6 copy-start.12
  380.3 3.0 copy-start.9
  380.3 3.2 copy-start.10
  380.3 3.4 copy-start.11
  380.3 3.6 copy-start.12
  429.7 3.0 copy-start.9
  429.7 3.2 copy-start.10
  429.7 3.4 copy-start.11
  429.7 3.6 copy-start.12
  479.1 3.0 copy-start.9
  479.1 3.2 copy-start.10
  479.1 3.4 copy-start.11
  479.1 3.6 copy-start.12
  (71 other events, 179.6 us)
where the time goes:
time: 520 us; the launch traced here: 516 us
  other arithmetic  294 us (57%)
  local copies, waits for them, and re-layouts  104 us (20%)
  waiting for transfers between devices  64.4 us (12%)
  loops' own time  30.7 us (6%)
  starting transfers between devices  19.6 us (4%)
    add x8, other arithmetic, pair_looks(): master_re * partner_re + master_im * partner_im  210 us
    ppermute x8, waiting for transfers between devices, shifted(): lax.ppermute(value, axis, [(source, source + steps) for source in range(l...  63.6 us
    another operation x32, local copies, waits for them, and re-layouts, pair_looks(): jnp.stack([master_re * partner_re + master_im * partner_im, master_im * p...  49.3 us
    convert_element_type x8, other arithmetic, pair_looks(): second_part = partner[:, :, t:t + column_count].astype(jnp.float32)  40.2 us
    another operation x1, loops' own time, shifted_pairs(): looks = lax.map(one_pair, jnp.arange(per_device * LAGS, dtype=jnp.int32))  30.7 us
    convert_element_type x8, other arithmetic, pair_looks(): first_part = master[:, :, t:t + column_count].astype(jnp.float32)  19.6 us
    ppermute x8, starting transfers between devices, shifted(): lax.ppermute(value, axis, [(source, source + steps) for source in range(l...  10.4 us
  transfers between devices with their start and end apart: 12, of which 9 were waited for; matrix products, arithmetic and copies ran while one was open for 3% of the time, Pallas kernels for 0%

commit v1 on v0

v1 whole, which is shorter than its diff:
```python
import functools

import jax
import jax.numpy as jnp
import numpy as np
from jax import lax
from jax.experimental import pallas as pl
from jax.experimental.pallas import tpu as pltpu
from jax.sharding import PartitionSpec as P

LAGS = 8
KERNELS = 16
TAPS = 8
FILTER_HALF = 8
FILTER_TAPS = 2 * FILTER_HALF + 1
LOOK_AZ = 4
LOOK_RG = 20
LANES = 128
META = 3
UNROLLED_PAIRS = 12


def up(value, unit):
    return -(-value // unit) * unit


def kernel_table():
    position = np.arange(TAPS) - 3.0 - np.arange(KERNELS)[:, None] / KERNELS
    shaped = np.sinc(position) * (0.5 + 0.5 * np.cos(np.pi * position / 5.0))
    table = np.zeros((KERNELS, LANES), np.float32)
    table[:, :TAPS] = shaped / shaped.sum(1, keepdims=True)
    return table


def lowpass_row(width):
    t = np.arange(FILTER_TAPS) - FILTER_HALF
    row = np.zeros((1, width), np.float32)
    row[0, :FILTER_TAPS] = 0.4 * np.sinc(0.4 * t) * (0.54 + 0.46 * np.cos(np.pi * t / (FILTER_HALF + 1)))
    return row


def halves(value):
    high = value.astype(jnp.bfloat16)
    return high, (value - high.astype(jnp.float32)).astype(jnp.bfloat16)


def dot(a, b):
    return jnp.dot(a, b, preferred_element_type=jnp.float32)


def dot_nt(a, b):
    return lax.dot_general(a, b, (((1,), (1,)), ((), ())), preferred_element_type=jnp.float32)


def pack_kernel(chunk, place_ref, offsets_ref, index_ref, slc_ref, before_ref, after_ref, out_ref, wide_ref):
    columns = slc_ref.shape[1]
    wide = out_ref.shape[2]
    first = place_ref[0] == 0
    last = place_ref[0] == place_ref[1] - 1
    zero = jnp.zeros_like(before_ref[...])
    wide_ref[:, :LANES] = jnp.where(first, zero, before_ref[...])
    wide_ref[:, LANES : LANES + columns] = slc_ref[...]
    wide_ref[:, LANES + columns :] = jnp.where(last, zero, after_ref[...])
    lane = lax.broadcasted_iota(jnp.int32, (slc_ref.shape[0], wide), 1)
    numbers = [offsets_ref[0, 0], index_ref[0, 0], index_ref[0, 1]]
    for j in range(out_ref.shape[0]):
        start = LANES + chunk * j - FILTER_HALF - 3 + offsets_ref[0, 1]
        tile = lax.shift_right_logical(start, 7)
        within = lax.bitwise_and(start, LANES - 1)
        window = wide_ref[:, pl.ds(pl.multiple_of(tile * LANES, LANES), wide + LANES)].astype(jnp.float32)
        moved = pltpu.roll(window, wide + LANES - within, 1)[:, :wide]
        for slot, number in enumerate(numbers):
            moved = jnp.where(lane == wide - META + slot, number.astype(jnp.float32), moved)
        out_ref[j] = moved.astype(jnp.bfloat16)


def picked_taps(table, index):
    row = lax.broadcasted_iota(jnp.int32, table.shape, 0).astype(jnp.float32)
    return jnp.sum(jnp.where(row == index, table, 0.0), axis=0, keepdims=True)


def banded(taps, distance):
    out = jnp.zeros(distance.shape, jnp.float32)
    for q in range(TAPS):
        out = jnp.where(distance == q, taps[:, q : q + 1], out)
    return out


def pairs_kernel(chunk, pairs, *refs):
    if isinstance(pairs, int):
        table_of_pairs, refs = refs[0], refs[1:]
    shift_ref, table_ref, lowpass_ref, recv_ref, out_ref, resampled_ref, weight_ref, product_ref = refs
    sources, rows, wide = recv_ref.shape
    dates = shift_ref.shape[0]
    az_count = sources // dates
    own_lines = rows // 2
    lines = own_lines * az_count
    groups = lines // LOOK_AZ
    looks = chunk // LOOK_RG
    table = table_ref[...]
    held = resampled_ref.shape[2]

    out_row = lax.broadcasted_iota(jnp.int32, (lines, lines), 0)
    in_row = lax.broadcasted_iota(jnp.int32, (lines, lines), 1)
    line = LOOK_AZ * (out_row % groups) + out_row // groups
    line_distance = (in_row - line + 3).astype(jnp.float32)
    span = min(2 * LANES, wide)
    column_distance = (
        lax.broadcasted_iota(jnp.int32, (span, LANES), 0) - lax.broadcasted_iota(jnp.int32, (span, LANES), 1)
    ).astype(jnp.float32)
    for date in range(dates):
        numbers = recv_ref[date * az_count, 0:16, wide - LANES :].astype(jnp.float32)[0:1, LANES - META :]
        line_offset, line_index, column_index = (numbers[:, s : s + 1] for s in range(META))
        line_taps = banded(picked_taps(table, line_index), line_distance - line_offset)
        line_taps = jnp.concatenate(halves(line_taps), axis=0)
        column_high, column_low = halves(banded(picked_taps(table, column_index), column_distance))
        moved = []
        for plane in range(2):
            rows_of = slice(plane * own_lines, (plane + 1) * own_lines)
            source = jnp.concatenate([recv_ref[date * az_count + a, rows_of, :] for a in range(az_count)], axis=0)
            both = dot(line_taps, source)
            moved.append(both[:lines] + both[lines:])
        moved_high, moved_low = halves(jnp.concatenate(moved, axis=0))
        for begin in range(0, held, LANES):
            end = min(begin + span, wide)
            taken = end - begin
            total = dot(moved_high[:, begin:end], column_high[:taken])
            total += dot(moved_low[:, begin:end], column_high[:taken])
            total += dot(moved_high[:, begin:end], column_low[:taken])
            resampled_ref[date, :, begin : begin + LANES] = total.astype(jnp.bfloat16)

    window = lowpass_ref[...]
    spacing = lax.broadcasted_iota(jnp.int32, window.shape, 1).astype(jnp.float32) - FILTER_HALF
    span = min(2 * LANES, held)

    def one_pair(place, own, other):
        gap = shift_ref[own] - shift_ref[other]
        angle = jnp.where(jnp.abs(spacing) <= FILTER_HALF, jnp.pi * gap * spacing, 0.0)
        for part, taps in enumerate((window * jnp.cos(angle), window * jnp.sin(angle))):
            spread = jnp.broadcast_to(taps, (LANES, 2 * LANES))
            spread = pltpu.roll(spread, 0, 1, stride=1, stride_axis=0)
            high, low = halves(spread)
            weight_ref[0, part * LANES : (part + 1) * LANES, :] = high
            weight_ref[1, part * LANES : (part + 1) * LANES, :] = low
        both = jnp.concatenate([resampled_ref[own], resampled_ref[other]], axis=0)
        for begin in range(0, up(chunk, LANES), LANES):
            end = min(begin + span, held)
            taken = end - begin
            total = dot_nt(both[:, begin:end], weight_ref[0, :, :taken])
            total += dot_nt(both[:, begin:end], weight_ref[1, :, :taken])
            cos, sin = total[:, :LANES], total[:, LANES:]
            re, im = slice(0, lines), slice(lines, 2 * lines)
            master_re = cos[re] + sin[im]
            master_im = cos[im] - sin[re]
            re, im = slice(2 * lines, 3 * lines), slice(3 * lines, 4 * lines)
            partner_re = cos[re] - sin[im]
            partner_im = cos[im] + sin[re]
            for part, product in enumerate(
                (
                    master_re * partner_re + master_im * partner_im,
                    master_im * partner_re - master_re * partner_im,
                )
            ):
                summed = sum(product[k * groups : (k + 1) * groups] for k in range(LOOK_AZ))
                product_ref[place, part, :, begin : begin + LANES] = summed

    if isinstance(pairs, int):
        count = pairs

        def step(place, carry):
            one_pair(place, table_of_pairs[place, 0], table_of_pairs[place, 1])
            return carry

        lax.fori_loop(0, count, step, 0)
    else:
        count = len(pairs)
        for place, (own, other) in enumerate(pairs):
            one_pair(place, own, other)

    out_width = out_ref.shape[2]
    column = lax.broadcasted_iota(jnp.int32, (product_ref.shape[3], out_width), 0)
    lane = lax.broadcasted_iota(jnp.int32, (product_ref.shape[3], out_width), 1)
    collect = jnp.where(column // LOOK_RG == lane % looks, 1.0, 0.0).astype(jnp.bfloat16)
    high, low = halves(product_ref[...].reshape(count * 2 * groups, product_ref.shape[3]))
    total = (dot(high, collect) + dot(low, collect)) * (1.0 / (LOOK_AZ * LOOK_RG))
    total = total.reshape(count, 2, groups, out_width)
    own_lane = lax.broadcasted_iota(jnp.int32, (groups, out_width), 1) // looks
    place = 0
    for own in range(dates):
        value = jnp.zeros((groups, out_width), jnp.float32)
        for lag in range(min(LAGS, dates - 1 - own)):
            for part in range(2):
                value = jnp.where(own_lane == lag * 2 + part, total[place, part], value)
            place += 1
        out_ref[own * az_count : (own + 1) * az_count] = value.reshape(az_count, groups // az_count, out_width)


def unpack_kernel(used_lags, looks, recv_ref, out_ref):
    sources, groups, width = recv_ref.shape
    columns = out_ref.shape[-1]
    lane = lax.broadcasted_iota(jnp.int32, (groups, columns), 1) // looks
    out_ref[...] = jnp.zeros_like(out_ref)
    for lag in range(used_lags):
        for part in range(2):
            value = jnp.zeros((groups, columns), jnp.float32)
            for source in range(sources):
                block = recv_ref[source]
                if width != columns:
                    block = block[:, :columns]
                shift = looks * (source - lag * 2 - part) % columns
                if shift:
                    block = pltpu.roll(block, shift, 1)
                value = jnp.where(lane == source, block, value)
            out_ref[part, lag] = value


def body(slc, offsets, kernel_index, range_shift):
    axes = ("date", "az")
    date_count, az_count, rng_count = (lax.axis_size(a) for a in ("date", "az", "rng"))
    peers = date_count * az_count
    lines, columns = slc.shape[2], slc.shape[3]
    dates = range_shift.shape[0]
    chunk = columns // peers
    looks = chunk // LOOK_RG
    groups = lines * az_count // LOOK_AZ
    wide = up(chunk + 2 * FILTER_HALF + TAPS - 1 + META, LANES)
    held = up(chunk + 2 * FILTER_HALF, LANES)
    used_lags = min(LAGS, dates - 1)
    out_width = up(used_lags * 2 * looks, LANES)
    vmem = pl.BlockSpec(memory_space=pltpu.VMEM)
    smem = pl.BlockSpec(memory_space=pltpu.SMEM)
    limit = pltpu.CompilerParams(vmem_limit_bytes=32 * 1024 * 1024)

    cells = slc.reshape(2 * lines, columns)
    place = lax.axis_index("rng")
    if rng_count == 2:
        edge = jnp.where(place == 0, cells[:, columns - LANES :], cells[:, :LANES])
        before = after = lax.ppermute(edge, "rng", [(0, 1), (1, 0)])
    else:
        forth = [(i, i + 1) for i in range(rng_count - 1)]
        before = lax.ppermute(cells[:, columns - LANES :], "rng", forth)
        after = lax.ppermute(cells[:, :LANES], "rng", [(b, a) for a, b in forth])

    packed = pl.pallas_call(
        functools.partial(pack_kernel, chunk),
        out_shape=jax.ShapeDtypeStruct((peers, 2 * lines, wide), jnp.bfloat16),
        in_specs=[smem] * 3 + [vmem] * 3,
        out_specs=vmem,
        scratch_shapes=[pltpu.VMEM((2 * lines, columns + 2 * LANES), jnp.bfloat16)],
        compiler_params=limit,
    )(jnp.stack([place, rng_count]).astype(jnp.int32), offsets, kernel_index, cells, before, after)
    arrived = lax.all_to_all(packed, axes, 0, 0, tiled=True)

    pairs = [(own, own + lag) for own in range(dates) for lag in range(1, LAGS + 1) if own + lag < dates]
    count = len(pairs)
    first = [jnp.asarray(np.array(pairs, np.int32))] if count > UNROLLED_PAIRS else []
    looked = pl.pallas_call(
        functools.partial(pairs_kernel, chunk, count if first else pairs),
        out_shape=jax.ShapeDtypeStruct((peers, groups // az_count, out_width), jnp.float32),
        in_specs=[smem] * len(first) + [smem] + [vmem] * 3,
        out_specs=vmem,
        scratch_shapes=[
            pltpu.VMEM((dates, 4 * (groups * LOOK_AZ) // 2, held), jnp.bfloat16),
            pltpu.VMEM((2, 2 * LANES, 2 * LANES), jnp.bfloat16),
            pltpu.VMEM((count, 2, groups, up(chunk, LANES)), jnp.float32),
        ],
        compiler_params=limit,
    )(*first, range_shift, jnp.asarray(kernel_table()), jnp.asarray(lowpass_row(2 * LANES)), arrived)
    returned = lax.all_to_all(looked, axes, 0, 0, tiled=True)

    out = pl.pallas_call(
        functools.partial(unpack_kernel, used_lags, looks),
        out_shape=jax.ShapeDtypeStruct((2, LAGS, groups // az_count, looks * peers), jnp.float32),
        in_specs=[vmem],
        out_specs=vmem,
        compiler_params=limit,
    )(returned)
    return out[:, None]


def solution(mesh):
    return jax.shard_map(
        body,
        mesh=mesh,
        in_specs=(
            P(None, ("groups", "date"), "az", "rng"),
            P(("groups", "date"), None),
            P(("groups", "date"), None),
            P("groups"),
        ),
        out_specs=P(None, ("groups", "date"), None, "az", "rng"),
        check_vma=False,
    )
```

time: 520 us -> 38.1 us (0.07)
  other arithmetic: 294 us -> 0.81 us
  local copies, waits for them, and re-layouts: 104 us -> 1 us
  waiting for transfers between devices: 64.4 us -> 1.64 us
  loops' own time: 30.7 us -> 0 us
  blocking collectives: 0 us -> 26 us
  starting transfers between devices: 19.6 us -> 2.94 us
  Pallas kernels: 0 us -> 5.34 us
    add x9 -> x0, other arithmetic: 217 us -> none  [the longest x8 210 us: pair_looks(): master_re * partner_re + master_im * partner_im]
    convert_element_type x18 -> x0, other arithmetic: 65.5 us -> none  [the longest x8 40.2 us: pair_looks(): second_part = partner[:, :, t:t + column_count].astype(jnp.float32)]
    ppermute x12 -> x1, waiting for transfers between devices: 64.4 us -> 1.64 us  [body(): before = after = lax.ppermute(edge, 'rng', [(0, 1), (1, 0)])]
    another operation x33 -> x0, local copies, waits for them, and re-layouts: 49.9 us -> none  [the longest x32 49.3 us: pair_looks(): jnp.stack([master_re * partner_re + master_im * partner_im, master_im * p...]
    another operation x1 -> x0, loops' own time: 30.7 us -> none  [shifted_pairs(): looks = lax.map(one_pair, jnp.arange(per_device * LAGS, dtype=jnp.int32))]
    all_to_all x0 -> x2, blocking collectives: none -> 26 us  [the longest x1 17.9 us: body(): arrived = lax.all_to_all(packed, axes, 0, 0, tiled=True)]
    dynamic_slice x24 -> x0, local copies, waits for them, and re-layouts: 19.5 us -> none  [the longest x8 9.65 us: one_pair(): lax.dynamic_index_in_dim(gathered, later, 1, keepdims=False)]
    ppermute x12 -> x1, starting transfers between devices: 19.6 us -> 2.94 us  [body(): before = after = lax.ppermute(edge, 'rng', [(0, 1), (1, 0)])]
  transfers between devices with their start and end apart: 12 -> 1, of which waited for: 9 -> 1; matrix products, arithmetic and copies ran while one was open for 3% -> 0% of each run, Pallas kernels for 0% -> 0%
where the time goes in v1:
time: 38.1 us; the launch traced here: 37.8 us
  blocking collectives  26 us (68%)
  Pallas kernels  5.34 us (14%)
  starting transfers between devices  2.94 us (8%)
  waiting for transfers between devices  1.64 us (4%)
  local copies, waits for them, and re-layouts  1 us (3%)
  other arithmetic  0.81 us (2%)
    all_to_all x1, blocking collectives, body(): arrived = lax.all_to_all(packed, axes, 0, 0, tiled=True)  17.9 us
    all_to_all x1, blocking collectives, body(): returned = lax.all_to_all(looked, axes, 0, 0, tiled=True)  8.12 us
    pallas_call x1, Pallas kernels, body(): pl.pallas_call(functools.partial(pairs_kernel, chunk, count if first else...  3.75 us
    ppermute x1, starting transfers between devices, body(): before = after = lax.ppermute(edge, 'rng', [(0, 1), (1, 0)])  2.94 us
    ppermute x1, waiting for transfers between devices, body(): before = after = lax.ppermute(edge, 'rng', [(0, 1), (1, 0)])  1.64 us
    unnamed x12, local copies, waits for them, and re-layouts  1 us
    pallas_call x1, Pallas kernels, body(): pl.pallas_call(functools.partial(pack_kernel, chunk), out_shape=jax.Shape...  0.86 us
  transfers between devices with their start and end apart: 1, of which 1 were waited for; matrix products, arithmetic and copies ran while one was open for 0% of the time, Pallas kernels for 0%

profile of v1, /device:TPU:0, one launch (start us, length us, event | category | flops | bytes accessed | tf_op | source)
XLA Modules:
  0.0 37.8 jit_solution(10525321690077833488)
XLA Ops:
  0.0 0.7 %slice_select_fusion = bf16[64,128]{1,0:T(8,128)(2,1)S(1)} fusion(bf16[64,2560]{1,0:T(8,128)(2,1)} %bitcast.5, pred[]{:T(512)S(6)} %eq.3), kind=kLoop, calls=%fused_computation | loop fusion | flops 8192 | bytes 49153 | tf_op jit(solution)/shard_map/jit(_where)/select_n | solution.py:237
  0.7 2.9 %collective-permute-start = (bf16[64,128]{1,0:T(8,128)(2,1)S(1)}, bf16[64,128]{1,0:T(8,128)(2,1)S(1)}, u32[]{:S(2)}, u32[]{:S(2)}) collective-permute-start(bf16[64,128]{1,0:T(8,128)(2,1)S(1)} %slice_select_fusion), channel_id=1, source_target_pairs={{0,2},{2,0},{1,3},{3,1},{4,6},{6,4},{5,7},{7,5},{8,10},{10,8},{9,1... | collective-permute-start | bytes 49160 | tf_op jit(solution)/shard_map/ppermute | solution.py:238
  3.7 0.0 copy-start.3
  3.7 0.0 copy-start.4
  3.7 0.1 pad_add_fusion.place_ref
  3.8 1.6 %collective-permute-done.before_ref.after_ref = bf16[64,128]{1,0:T(8,128)(2,1)S(1)} collective-permute-done((bf16[64,128]{1,0:T(8,128)(2,1)S(1)}, bf16[64,128]{1,0:T(8,128)(2,1)S(1)}, u32[]{:S(2)}, u32[]{:S(2)}) %collective-permute-start) | collective-permute-done | bytes 16416 | tf_op jit(solution)/shard_map/ppermute | solution.py:238
  5.4 0.0 copy-done.3
  5.4 0.0 copy-done.4
  5.4 0.0 copy-start
  5.4 1.0 %copy-done = bf16[2,1,32,2560]{3,2,1,0:T(8,128)(2,1)S(1)} copy-done((bf16[2,1,32,2560]{3,2,1,0:T(8,128)(2,1)S(1)}, bf16[2,1,32,2560]{3,2,1,0:T(8,128)(2,1)}, u32[]{:S(2)}) %copy-start) | copy-done | bytes 327704
  6.4 0.9 %shard_map.64 = bf16[8,64,384]{2,1,0:T(8,128)(2,1)S(1)} custom-call(s32[2]{0:T(128)S(1)} %pad_add_fusion.place_ref, s32[1,2]{1,0:T(1,128)S(1)} %copy-done.3, s32[1,2]{1,0:T(1,128)S(1)} %copy-done.4, bf16[64,2560]{1,0:T(8,128)(2,1)S(1)} %bitcast.6, bf16[64,128]{1,0:T(8,128)(2,1)S(1)} %collective-permute-done.before_ref.after_ref, ...), custom_call_target="tpu_custom_call" | custom-call | tf_op jit(solution)/shard_map/pallas_call | solution.py:244
  7.2 0.0 copy-start.1
  7.3 0.0 copy-start.2
  7.3 0.0 copy-start.5
  7.3 17.9 %all_to_all.10.refs_3_ = bf16[8,64,384]{2,1,0:T(8,128)(2,1)S(1)} all-to-all(bf16[8,64,384]{2,1,0:T(8,128)(2,1)S(1)} %shard_map.64), channel_id=1, replica_groups=mesh['groups'=2,'date'=4,'rng'=2,'az'=2] {'date','az'}, dimensions={0} | all-to-all | bytes 786432 | tf_op jit(solution)/shard_map/all_to_all | solution.py:252
  25.2 0.0 copy-done.1
  25.2 0.0 copy-done.2
  25.2 0.0 copy-done.5
  25.2 3.7 %shard_map.65 = f32[8,8,128]{2,1,0:T(8,128)S(1)} custom-call(f32[4]{0:T(128)S(1)} %copy-done.5, f32[16,128]{1,0:T(8,128)S(1)} %copy-done.1, f32[1,256]{1,0:T(1,128)S(1)} %copy-done.2, bf16[8,64,384]{2,1,0:T(8,128)(2,1)S(1)} %all_to_all.10.refs_3_), custom_call_target="tpu_custom_call" | custom-call | tf_op jit(solution)/shard_map/pallas_call | solution.py:257
  28.9 8.1 %all_to_all.11.recv_ref = f32[8,8,128]{2,1,0:T(8,128)S(1)} all-to-all(f32[8,8,128]{2,1,0:T(8,128)S(1)} %shard_map.65), channel_id=1, replica_groups=mesh['groups'=2,'date'=4,'rng'=2,'az'=2] {'date','az'}, dimensions={0} | all-to-all | bytes 65536 | tf_op jit(solution)/shard_map/all_to_all | solution.py:269
  37.0 0.7 %shard_map.66 = f32[2,8,8,128]{3,2,1,0:T(8,128)} custom-call(f32[8,8,128]{2,1,0:T(8,128)S(1)} %all_to_all.11.recv_ref), custom_call_target="tpu_custom_call" | custom-call | tf_op jit(solution)/shard_map/pallas_call | solution.py:271
Async XLA Ops:
  0.7 4.7 %collective-permute-start = (bf16[64,128]{1,0:T(8,128)(2,1)S(1)}, bf16[64,128]{1,0:T(8,128)(2,1)S(1)}, u32[]{:S(2)}, u32[]{:S(2)}) collective-permute-start(bf16[64,128]{1,0:T(8,128)(2,1)S(1)} %slice_select_fusion), channel_id=1, source_target_pairs={{0,2},{2,0},{1,3},{3,1},{4,6},{6,4},{5,7},{7,5},{8,10},{10,8},{9,1... | collective-permute-start | bytes 49160 | tf_op jit(solution)/shard_map/ppermute | solution.py:238
  3.7 1.7 %copy-start.3 = (s32[1,2]{1,0:T(1,128)S(1)}, s32[1,2]{1,0:T(1,128)}, u32[]{:S(2)}) copy-start(s32[1,2]{1,0:T(1,128)} %offsets_ref.1) | copy-start | bytes 28
  3.7 1.7 %copy-start.4 = (s32[1,2]{1,0:T(1,128)S(1)}, s32[1,2]{1,0:T(1,128)}, u32[]{:S(2)}) copy-start(s32[1,2]{1,0:T(1,128)} %index_ref.1) | copy-start | bytes 28
  5.4 1.0 %copy-start = (bf16[2,1,32,2560]{3,2,1,0:T(8,128)(2,1)S(1)}, bf16[2,1,32,2560]{3,2,1,0:T(8,128)(2,1)}, u32[]{:S(2)}) copy-start(bf16[2,1,32,2560]{3,2,1,0:T(8,128)(2,1)} %param.6) | copy-start | bytes 983044
  7.2 17.9 %copy-start.1 = (f32[16,128]{1,0:T(8,128)S(1)}, f32[16,128]{1,0:T(8,128)}, u32[]{:S(2)}) copy-start(f32[16,128]{1,0:T(8,128)} %constant.12.clone.refs_1_) | copy-start | bytes 24580
  7.3 17.9 %copy-start.2 = (f32[1,256]{1,0:T(1,128)S(1)}, f32[1,256]{1,0:T(1,128)}, u32[]{:S(2)}) copy-start(f32[1,256]{1,0:T(1,128)} %constant.13.clone.refs_2_) | copy-start | bytes 3076
  7.3 17.9 %copy-start.5 = (f32[4]{0:T(128)S(1)}, f32[4]{0:T(128)}, u32[]{:S(2)}) copy-start(f32[4]{0:T(128)} %refs_0_.1) | copy-start | bytes 52
